TPU v7x, 512 devices: a whole 4x8x8 slice. The times are simulated.
512 devices in a mesh: users: 64 (over y, z_hi, x), cand: 8 (over z_lo, core).
Axes of the slice: x: 4, y: 8, z: 8 (z_hi: 2, z_lo: 4; z = z_hi * 4 + z_lo), core: 2. Of those that a mesh axis runs over, the one named last changes fastest.
Arguments:
- candidate_rows: bfloat16 [32768, 1024], P(('users', 'cand')), may hold values from -6 to 6
- weight_in: bfloat16 [2, 1024, 8, 512], P(None, None, 'cand'), may hold values from -0.1875 to 0.1875
- weight_out: bfloat16 [2, 8, 128, 1024], P(None, 'cand'), may hold values from -0.1875 to 0.1875
- history_cache: bfloat16 [2, 2, 8192, 8, 128], P(None, None, 'users', 'cand'), may hold values from -6 to 6
- block_user: int32 [64], replicated, may hold values from 0 to 15, as said below
- block_offset: int32 [64], replicated, may hold values from 0 to 31, as said below
- history_length: int32 [16], replicated, may hold values from 1 to 4096, as said below
- candidate_count: int32 [16], replicated, may hold values from 1 to 16384, as said below
Outputs:
- scored_rows: bfloat16 [32768, 1024], P(('users', 'cand'))
Inputs may be any that keep to these rules, and one draw needn't show every extreme that they name: `block_user`: every one of the 16 users owns at least one block; the blocks of one user may stand anywhere; exactly one user owns 64 / 2 blocks, every other user fewer. `block_offset`: the blocks of a user that owns b blocks carry the offsets 0 to b - 1, each once. `history_length`: a user that owns b blocks has more than (b - 1) * 128 and at most b * 128 history rows. `candidate_count`: the counts sum to 32768; the rows of one user are consecutive, users in increasing order.
All inputs are finite; a program needn't handle non-finite values.
Results may differ from a plain program's by a relative error of at most 0.027.
Values may be sent and summed in bfloat16 or wider, within the bound.
A program may use at most 64 MiB of HBM per device.

v0:
```python
import math
import jax
import jax.numpy as jnp
from jax import lax
from jax.sharding import PartitionSpec as P

BLOCK = 128


def body(
    candidate_rows,
    weight_in,
    weight_out,
    history_cache,
    block_user,
    block_offset,
    history_length,
    candidate_count,
):
    own_rows, model_width = candidate_rows.shape
    layers, model_again, heads_here, packed = weight_in.shape
    head_dim = packed // 4
    cand_devices = lax.axis_size("cand")
    row_count = own_rows * cand_devices
    score_scale = 1.0 / math.sqrt(head_dim)
    user_count = history_length.shape[0]
    users_all = jnp.arange(user_count, dtype=jnp.int32)
    user_ends = jnp.cumsum(candidate_count)
    group_rows = lax.axis_index("users") * row_count + jnp.arange(row_count, dtype=jnp.int32)
    cand_user = jnp.sum((group_rows[:, None] >= user_ends[None, :]).astype(jnp.int32), axis=1)
    step_rows = 4 * BLOCK

    def block_term(accumulated, key_value, piece_start, queries):
        span_rows = key_value.shape[1]
        span_blocks = span_rows // BLOCK
        first_block = piece_start // BLOCK
        owners = lax.dynamic_slice_in_dim(block_user, first_block, span_blocks)
        places = lax.dynamic_slice_in_dim(block_offset, first_block, span_blocks)
        row_user = jnp.broadcast_to(owners[:, None], (span_blocks, BLOCK)).reshape(span_rows)
        row_place = (places[:, None] * BLOCK + jnp.arange(BLOCK, dtype=jnp.int32)[None, :]).reshape(
            span_rows
        )
        row_length = jnp.sum(
            jnp.where(row_user[:, None] == users_all[None, :], history_length[None, :], 0), axis=1
        )
        visible = (cand_user[:, None] == row_user[None, :]) & (row_place < row_length)[None, :]
        scores = (
            jnp.einsum("rhd,nhd->hrn", queries, key_value[0], preferred_element_type=jnp.float32)
            * score_scale
        )
        weights = jnp.where(visible[None], jax.nn.silu(scores), 0.0).astype(jnp.bfloat16)
        return accumulated + jnp.einsum(
            "hrn,nhd->rhd", weights, key_value[1], preferred_element_type=jnp.float32
        )

    current_own = candidate_rows
    for layer_index in range(layers):
        project_segment = lax.all_gather(current_own, "cand", axis=0, tiled=True)
        flat = weight_in[layer_index].reshape(model_width, heads_here * packed)
        mixed = jnp.dot(project_segment, flat, preferred_element_type=jnp.float32)
        projected = (
            jax.nn.silu(mixed)
            .astype(jnp.bfloat16)
            .reshape(project_segment.shape[0], heads_here, 4, head_dim)
        )
        gate_part = projected[:, :, 0]
        values_part = projected[:, :, 1]
        queries = projected[:, :, 2]
        keys_part = projected[:, :, 3]
        own_score = (
            jnp.sum(queries.astype(jnp.float32) * keys_part.astype(jnp.float32), axis=-1)
            * score_scale
        )
        own_weight = jax.nn.silu(own_score).astype(jnp.bfloat16)
        own_term = own_weight.astype(jnp.float32)[..., None] * values_part.astype(jnp.float32)
        empty_sum = jnp.zeros((row_count, heads_here, head_dim), jnp.float32)
        segment = lax.all_gather(history_cache[layer_index], "users", axis=1, tiled=True)
        fold_span_rows = segment.shape[1]
        turns = fold_span_rows // step_rows

        def advance(position, running):
            sliced = lax.dynamic_slice_in_dim(segment, position * step_rows, step_rows, 1)
            return block_term(running, sliced, position * step_rows, queries)

        attended = lax.fori_loop(0, turns, advance, empty_sum)
        attended = attended + own_term
        centred = attended - jnp.mean(attended, axis=-1, keepdims=True)
        variance = jnp.mean(centred * centred, axis=-1, keepdims=True)
        gated = (centred * lax.rsqrt(variance + 1e-05) * gate_part.astype(jnp.float32)).astype(
            jnp.bfloat16
        )
        partial_out = jnp.dot(
            gated.reshape(row_count, heads_here * head_dim),
            weight_out[layer_index].reshape(heads_here * head_dim, model_width),
            preferred_element_type=jnp.float32,
        )
        shared = lax.psum_scatter(
            partial_out.astype(jnp.bfloat16), "cand", scatter_dimension=0, tiled=True
        ).astype(jnp.float32)
        current_own = (current_own.astype(jnp.float32) + shared).astype(jnp.bfloat16)
    return current_own


def solution(mesh):
    placed = (
        P(("users", "cand"), None),
        P(None, None, "cand", None),
        P(None, "cand", None, None),
        P(None, None, "users", "cand", None),
        P(),
        P(),
        P(),
        P(),
    )
    return jax.shard_map(
        body, mesh=mesh, in_specs=placed, out_specs=P(("users", "cand"), None), check_vma=False
    )
```

profile of v0, /device:TPU:2, one launch (start us, length us, event | category | flops | bytes accessed | tf_op | source)
XLA Modules:
  0.0 570.2 jit_solution(17218734392977073218)
XLA Ops:
  9.9 44.5 %all-gather.7.cloned.1.call-done = bf16[512,1024]{1,0:T(8,128)(2,1)} async-done(((bf16[64,1024]{1,0:T(8,128)(2,1)}), bf16[512,1024]{1,0:T(8,128)(2,1)}) %all-gather.7.cloned.1.call-update) | async-done | bytes 1048592 | tf_op jit(solution)/shard_map/all_gather | solution.py:58
  54.4 2.4 multiply_convert_fusion.1
  57.1 159.0 %all-gather.11.cloned.1.call-done = bf16[1,2,8192,1,128]{4,2,1,3,0:T(8,128)(2,1)} async-done(((bf16[1,2,128,1,128]{4,2,1,3,0:T(8,128)(2,1)}), bf16[1,2,8192,1,128]{4,2,1,3,0:T(8,128)(2,1)}) %all-gather.11.cloned.1.call-update) | async-done | bytes 4194320 | tf_op jit(solution)/shard_map/all_gather | solution.py:77
  216.1 35.4 %while.32 = (s32[]{:T(128)}, f32[512,1,128]{0,2,1:T(8,128)S(1)}, bf16[2,8192,1,128]{3,1,2,0:T(8,128)(2,1)}, s32[512]{0:T(512)S(1)}, s32[64]{0:T(128)S(1)}, /*ind...) while((s32[]{:T(128)}, f32[512,1,128]{0,2,1:T(8,128)S(1)}, ...), condition=%wide.region_4.5_spmd.clone, body=%wide.region_2.4_spmd.clone.sunk | while | flops 136733216 | bytes 933431 | solution.py:85
  218.7 1.8 fusion.82
  225.4 1.8 fusion.82
  227.6 1.8 fusion.82
  234.2 1.8 fusion.82
  236.4 1.8 fusion.82
  253.2 34.7 %reduce-scatter.3.cloned.1.call-done = bf16[64,1024]{1,0:T(8,128)(2,1)} async-done(((bf16[512,1024]{1,0:T(8,128)(2,1)}), bf16[64,1024]{1,0:T(8,128)(2,1)}) %reduce-scatter.3.cloned.1.call-update) | async-done | bytes 131088 | tf_op jit(solution)/shard_map/reduce_scatter | solution.py:97
  290.1 38.4 %all-gather.9.cloned.1.call-done = bf16[512,1024]{1,0:T(8,128)(2,1)} async-done(((bf16[64,1024]{1,0:T(8,128)(2,1)}), bf16[512,1024]{1,0:T(8,128)(2,1)}) %all-gather.9.cloned.1.call-update) | async-done | bytes 1048592 | tf_op jit(solution)/shard_map/all_gather | solution.py:58
  328.5 2.4 multiply_convert_fusion
  331.1 158.8 %all-gather.13.cloned.1.call-done = bf16[1,2,8192,1,128]{4,2,1,3,0:T(8,128)(2,1)} async-done(((bf16[1,2,128,1,128]{4,2,1,3,0:T(8,128)(2,1)}), bf16[1,2,8192,1,128]{4,2,1,3,0:T(8,128)(2,1)}) %all-gather.13.cloned.1.call-update) | async-done | bytes 4194320 | tf_op jit(solution)/shard_map/all_gather | solution.py:77
  490.0 35.3 %while.33 = (s32[]{:T(128)}, f32[512,1,128]{0,2,1:T(8,128)S(1)}, bf16[2,8192,1,128]{3,1,2,0:T(8,128)(2,1)}, s32[512]{0:T(512)S(1)}, s32[64]{0:T(128)S(1)}, /*ind...) while((s32[]{:T(128)}, f32[512,1,128]{0,2,1:T(8,128)S(1)}, ...), condition=%wide.region_11.12_spmd.clone, body=%wide.region_9.11_spmd.clone.sunk | while | flops 136733216 | bytes 933431 | solution.py:85
  490.4 1.8 fusion.84
  492.6 1.8 fusion.84
  497.0 1.8 fusion.84
  501.4 1.8 fusion.84
  505.8 1.8 fusion.84
  510.3 1.8 fusion.84
  514.7 1.8 fusion.84
  519.1 1.8 fusion.84
  523.5 1.8 fusion.84
  527.0 34.8 %reduce-scatter.5.cloned.1.call-done = bf16[64,1024]{1,0:T(8,128)(2,1)} async-done(((bf16[512,1024]{1,0:T(8,128)(2,1)}), bf16[64,1024]{1,0:T(8,128)(2,1)}) %reduce-scatter.5.cloned.1.call-update) | async-done | bytes 131088 | tf_op jit(solution)/shard_map/reduce_scatter | solution.py:97
  (230 shorter events, 55.1 us)
Async XLA Ops:
  6.5 47.9 %all-gather.7.cloned.1.call-start = ((), (), s32[]{:S(2)}) async-start(), calls=%async_computation.2 | async-start | bytes 1179648 | tf_op jit(solution)/shard_map/all_gather | solution.py:58
  7.3 208.8 %all-gather.11.cloned.1.call-start = ((), (), s32[]{:S(2)}) async-start(), calls=%async_computation.6 | async-start | bytes 4259840 | tf_op jit(solution)/shard_map/all_gather | solution.py:77
  8.9 279.0 %reduce-scatter.3.cloned.1.call-start = ((), (), s32[]{:S(2)}) async-start(), calls=%async_computation.3 | async-start | bytes 1179648 | tf_op jit(solution)/shard_map/reduce_scatter | solution.py:97
  9.9 206.2 %copy-start.3 = (s32[16]{0:T(128)S(1)}, s32[16]{0:T(128)}, u32[]{:S(2)}) copy-start(s32[16]{0:T(128)} %param.18) | copy-start | bytes 196
  9.9 206.2 %copy-start.4 = (s32[64]{0:T(128)S(1)}, s32[64]{0:T(128)}, u32[]{:S(2)}) copy-start(s32[64]{0:T(128)} %param.16) | copy-start | bytes 772
  9.9 206.2 %copy-start.5 = (s32[64]{0:T(128)S(1)}, s32[64]{0:T(128)}, u32[]{:S(2)}) copy-start(s32[64]{0:T(128)} %param.17) | copy-start | bytes 772
  216.1 35.5 %copy-start.2 = (bf16[2,1,128,1024]{3,2,1,0:T(8,128)(2,1)S(1)}, bf16[2,1,128,1024]{3,2,1,0:T(8,128)(2,1)}, u32[]{:S(2)}) copy-start(bf16[2,1,128,1024]{3,2,1,0:T(8,128)(2,1)} %param.14) | copy-start | bytes 1572868
  216.1 71.8 %copy-start.1 = (bf16[64,1024]{1,0:T(8,128)(2,1)S(1)}, bf16[64,1024]{1,0:T(8,128)(2,1)}, u32[]{:S(2)}) copy-start(bf16[64,1024]{1,0:T(8,128)(2,1)} %param.12) | copy-start | bytes 393220
  253.1 75.4 %all-gather.9.cloned.1.call-start = ((), (), s32[]{:S(2)}) async-start(), calls=%async_computation.4 | async-start | bytes 1179648 | tf_op jit(solution)/shard_map/all_gather | solution.py:58
  289.5 200.5 %all-gather.13.cloned.1.call-start = ((), (), s32[]{:S(2)}) async-start(), calls=%async_computation.7 | async-start | bytes 4259840 | tf_op jit(solution)/shard_map/all_gather | solution.py:77
  290.1 271.7 %reduce-scatter.5.cloned.1.call-start = ((), (), s32[]{:S(2)}) async-start(), calls=%async_computation.5 | async-start | bytes 1179648 | tf_op jit(solution)/shard_map/reduce_scatter | solution.py:97
  490.0 71.8 %copy-start = (bf16[64,1024]{1,0:T(8,128)(2,1)S(1)}, bf16[64,1024]{1,0:T(8,128)(2,1)}, u32[]{:S(2)}) copy-start(bf16[64,1024]{1,0:T(8,128)(2,1)} %add_convert_fusion.1) | copy-start | bytes 393220
Sparse Core Ops, SparseCore 0:
  9.4 44.9 all-gather.6
  58.8 157.2 all-gather.10
  253.2 34.5 reduce-scatter.2
  289.8 38.6 all-gather.8
  332.7 157.2 all-gather.12
  527.1 34.6 reduce-scatter.4
where the time goes:
time: 571 us; the launch traced here: 570 us
  waiting for transfers between devices  471 us (82%)
  matrix products  64.3 us (11%)
  between operations  13.6 us (2%)
  other arithmetic  11.6 us (2%)
  local copies, waits for them, and re-layouts  7.34 us (1%)
    all_gather x2, waiting for transfers between devices, body(): lax.all_gather(history_cache[layer_index], 'users', axis=1, tiled=True)  318 us
    all_gather x2, waiting for transfers between devices, body(): project_segment = lax.all_gather(current_own, 'cand', axis=0, tiled=True)  82.9 us
    reduce_scatter x2, waiting for transfers between devices, body(): lax.psum_scatter(partial_out.astype(jnp.bfloat16), 'cand', scatter_dimens...  69.5 us
    dot_general x32, matrix products, block_term(): jnp.einsum('hrn,nhd->rhd', weights, key_value[1], preferred_element_type=...  56.5 us
  transfers between devices with their start and end apart: 6, of which 6 were waited for; matrix products, arithmetic and copies ran while one was open for 1% of the time, Pallas kernels for 0%

commit v1 on v0

--- a/solution.py
+++ b/solution.py
@@ -74,7 +74,12 @@
         own_weight = jax.nn.silu(own_score).astype(jnp.bfloat16)
         own_term = own_weight.astype(jnp.float32)[..., None] * values_part.astype(jnp.float32)
         empty_sum = jnp.zeros((row_count, heads_here, head_dim), jnp.float32)
-        segment = lax.all_gather(history_cache[layer_index], "users", axis=1, tiled=True)
+        segment = jnp.concatenate(
+            lax.all_to_all(
+                jnp.stack([history_cache[layer_index]] * lax.axis_size("users")), "users", 0, 0
+            ),
+            axis=1,
+        )
         fold_span_rows = segment.shape[1]
         turns = fold_span_rows // step_rows
 

time: 571 us -> 408 us (0.71)
  waiting for transfers between devices: 471 us -> 258 us
  starting transfers between devices: 0.2 us -> 36.1 us
  local copies, waits for them, and re-layouts: 7.34 us -> 21.5 us
    all_gather x2 -> x0, waiting for transfers between devices: 318 us -> none  [body(): lax.all_gather(history_cache[layer_index], 'users', axis=1, tiled=True)]
    all_gather x2, waiting for transfers between devices: 82.9 us -> 146 us  [body(): project_segment = lax.all_gather(current_own, 'cand', axis=0, tiled=True)]
    reduce_scatter x2, waiting for transfers between devices: 69.5 us -> 111 us  [body(): lax.psum_scatter(partial_out.astype(jnp.bfloat16), 'cand', scatter_dimens...]
    all_to_all x0 -> x2, starting transfers between devices: none -> 35.9 us  [body(): lax.all_to_all(jnp.stack([history_cache[layer_index]] * lax.axis_size('us...]
    all_to_all x0 -> x2, local copies, waits for them, and re-layouts: none -> 9.48 us  [body(): lax.all_to_all(jnp.stack([history_cache[layer_index]] * lax.axis_size('us...]
  transfers between devices with their start and end apart: 6 -> 6, of which waited for: 6 -> 4; matrix products, arithmetic and copies ran while one was open for 1% -> 12% of each run, Pallas kernels for 0% -> 0%
where the time goes in v1:
time: 408 us; the launch traced here: 407 us
  waiting for transfers between devices  258 us (63%)
  matrix products  64.3 us (16%)
  starting transfers between devices  36.1 us (9%)
  local copies, waits for them, and re-layouts  21.5 us (5%)
  between operations  13.3 us (3%)
  other arithmetic  11.6 us (3%)
    all_gather x2, waiting for transfers between devices, body(): project_segment = lax.all_gather(current_own, 'cand', axis=0, tiled=True)  146 us
    reduce_scatter x2, waiting for transfers between devices, body(): lax.psum_scatter(partial_out.astype(jnp.bfloat16), 'cand', scatter_dimens...  111 us
    dot_general x32, matrix products, block_term(): jnp.einsum('hrn,nhd->rhd', weights, key_value[1], preferred_element_type=...  56.4 us
    all_to_all x2, starting transfers between devices, body(): lax.all_to_all(jnp.stack([history_cache[layer_index]] * lax.axis_size('us...  35.9 us
    all_to_all x2, local copies, waits for them, and re-layouts, body(): lax.all_to_all(jnp.stack([history_cache[layer_index]] * lax.axis_size('us...  9.48 us
  transfers between devices with their start and end apart: 6, of which 4 were waited for; matrix products, arithmetic and copies ran while one was open for 12% of the time, Pallas kernels for 0%

profile of v1, /device:TPU:2, one launch (start us, length us, event | category | flops | bytes accessed | tf_op | source)
XLA Modules:
  0.0 406.6 jit_solution(12979235742452881655)
XLA Ops:
  7.4 3.0 stack.6
  10.4 19.4 %all-to-all-start = ((bf16[64,2,128,1,128]{4,2,1,3,0:T(8,128)(2,1)}), bf16[64,2,128,1,128]{4,2,1,3,0:T(8,128)(2,1)}, u32[]{:S(2)}, u32[]{:S(2)}) async-start(bf16[64,2,128,1,128]{4,2,1,3,0:T(8,128)(2,1)} %stack.6), calls=%async_computation | async-start | bytes 8388608 | tf_op jit(solution)/shard_map/all_to_all | solution.py:78
  30.9 109.4 %all-gather.3.cloned.1.call-done = bf16[512,1024]{1,0:T(8,128)(2,1)} async-done(((bf16[64,1024]{1,0:T(8,128)(2,1)}), bf16[512,1024]{1,0:T(8,128)(2,1)}) %all-gather.3.cloned.1.call-update) | async-done | bytes 1048592 | tf_op jit(solution)/shard_map/all_gather | solution.py:58
  140.3 2.4 multiply_convert_fusion.1
  143.0 3.0 stack.7
  146.0 16.5 %all-to-all-start.1 = ((bf16[64,2,128,1,128]{4,2,1,3,0:T(8,128)(2,1)}), bf16[64,2,128,1,128]{4,2,1,3,0:T(8,128)(2,1)}, u32[]{:S(2)}, u32[]{:S(2)}) async-start(bf16[64,2,128,1,128]{4,2,1,3,0:T(8,128)(2,1)} %stack.7), calls=%async_computation.2 | async-start | bytes 8388608 | tf_op jit(solution)/shard_map/all_to_all | solution.py:78
  162.6 4.7 %copy.24 = bf16[64,2,128,1,128]{4,2,0,1,3:T(8,128)(2,1)} copy(bf16[64,2,128,1,128]{4,2,1,3,0:T(8,128)(2,1)} %all-to-all-done) | data formatting | bytes 8388608 | tf_op jit(solution)/shard_map/all_to_all | solution.py:78
  167.4 35.3 %while.32 = (s32[]{:T(128)}, f32[512,1,128]{0,2,1:T(8,128)S(1)}, bf16[2,8192,1,128]{3,1,2,0:T(8,128)(2,1)}, s32[512]{0:T(512)S(1)}, s32[64]{0:T(128)S(1)}, /*ind...) while((s32[]{:T(128)}, f32[512,1,128]{0,2,1:T(8,128)S(1)}, ...), condition=%wide.region_4.5_spmd.clone, body=%wide.region_2.4_spmd.clone.sunk | while | flops 136733216 | bytes 933431 | solution.py:90
  176.7 1.8 fusion.81
  185.5 1.8 fusion.81
  194.3 1.8 fusion.81
  204.5 71.1 %reduce-scatter.3.cloned.1.call-done = bf16[64,1024]{1,0:T(8,128)(2,1)} async-done(((bf16[512,1024]{1,0:T(8,128)(2,1)}), bf16[64,1024]{1,0:T(8,128)(2,1)}) %reduce-scatter.3.cloned.1.call-update) | async-done | bytes 131088 | tf_op jit(solution)/shard_map/reduce_scatter | solution.py:102
  277.3 4.7 %copy.28 = bf16[64,2,128,1,128]{4,2,0,1,3:T(8,128)(2,1)} copy(bf16[64,2,128,1,128]{4,2,1,3,0:T(8,128)(2,1)} %all-to-all-done.1) | data formatting | bytes 8388608 | tf_op jit(solution)/shard_map/all_to_all | solution.py:78
  282.1 37.0 %all-gather.5.cloned.1.call-done = bf16[512,1024]{1,0:T(8,128)(2,1)} async-done(((bf16[64,1024]{1,0:T(8,128)(2,1)}), bf16[512,1024]{1,0:T(8,128)(2,1)}) %all-gather.5.cloned.1.call-update) | async-done | bytes 1048592 | tf_op jit(solution)/shard_map/all_gather | solution.py:58
  319.1 2.4 multiply_convert_fusion
  321.7 35.4 %while.33 = (s32[]{:T(128)}, f32[512,1,128]{0,2,1:T(8,128)S(1)}, bf16[2,8192,1,128]{3,1,2,0:T(8,128)(2,1)}, s32[512]{0:T(512)S(1)}, s32[64]{0:T(128)S(1)}, /*ind...) while((s32[]{:T(128)}, f32[512,1,128]{0,2,1:T(8,128)S(1)}, ...), condition=%wide.region_11.12_spmd.clone, body=%wide.region_9.11_spmd.clone.sunk | while | flops 136733216 | bytes 933431 | solution.py:90
  328.8 1.8 fusion.83
  333.2 1.8 fusion.83
  337.6 1.8 fusion.83
  342.1 1.8 fusion.83
  346.5 1.8 fusion.83
  350.9 1.8 fusion.83
  355.3 1.8 fusion.83
  358.8 39.7 %reduce-scatter.5.cloned.1.call-done = bf16[64,1024]{1,0:T(8,128)(2,1)} async-done(((bf16[512,1024]{1,0:T(8,128)(2,1)}), bf16[64,1024]{1,0:T(8,128)(2,1)}) %reduce-scatter.5.cloned.1.call-update) | async-done | bytes 131088 | tf_op jit(solution)/shard_map/reduce_scatter | solution.py:102
  (234 shorter events, 60.3 us)
Async XLA Ops:
  10.4 20.2 %copy-start.4 = (s32[16]{0:T(128)S(1)}, s32[16]{0:T(128)}, u32[]{:S(2)}) copy-start(s32[16]{0:T(128)} %param.19) | copy-start | bytes 196
  10.4 132.6 %all-to-all-start = ((bf16[64,2,128,1,128]{4,2,1,3,0:T(8,128)(2,1)}), bf16[64,2,128,1,128]{4,2,1,3,0:T(8,128)(2,1)}, u32[]{:S(2)}, u32[]{:S(2)}) async-start(bf16[64,2,128,1,128]{4,2,1,3,0:T(8,128)(2,1)} %stack.6), calls=%async_computation | async-start | bytes 8388608 | tf_op jit(solution)/shard_map/all_to_all | solution.py:78
  29.8 110.5 %all-gather.3.cloned.1.call-start = ((), (), s32[]{:S(2)}) async-start(), calls=%async_computation.4 | async-start | bytes 1179648 | tf_op jit(solution)/shard_map/all_gather | solution.py:58
  146.0 131.3 %all-to-all-start.1 = ((bf16[64,2,128,1,128]{4,2,1,3,0:T(8,128)(2,1)}), bf16[64,2,128,1,128]{4,2,1,3,0:T(8,128)(2,1)}, u32[]{:S(2)}, u32[]{:S(2)}) async-start(bf16[64,2,128,1,128]{4,2,1,3,0:T(8,128)(2,1)} %stack.7), calls=%async_computation.2 | async-start | bytes 8388608 | tf_op jit(solution)/shard_map/all_to_all | solution.py:78
  162.5 4.8 %copy-start.3 = (s32[16]{0:T(128)S(1)}, s32[16]{0:T(128)}, u32[]{:S(2)}) copy-start(s32[16]{0:T(128)} %param.18) | copy-start | bytes 196
  162.5 4.8 %copy-start.5 = (s32[64]{0:T(128)S(1)}, s32[64]{0:T(128)}, u32[]{:S(2)}) copy-start(s32[64]{0:T(128)} %param.16) | copy-start | bytes 772
  162.6 4.8 %copy-start.6 = (s32[64]{0:T(128)S(1)}, s32[64]{0:T(128)}, u32[]{:S(2)}) copy-start(s32[64]{0:T(128)} %param.17) | copy-start | bytes 772
  162.6 113.1 %reduce-scatter.3.cloned.1.call-start = ((), (), s32[]{:S(2)}) async-start(), calls=%async_computation.5 | async-start | bytes 1179648 | tf_op jit(solution)/shard_map/reduce_scatter | solution.py:102
  167.4 35.5 %copy-start.2 = (bf16[2,1,128,1024]{3,2,1,0:T(8,128)(2,1)S(1)}, bf16[2,1,128,1024]{3,2,1,0:T(8,128)(2,1)}, u32[]{:S(2)}) copy-start(bf16[2,1,128,1024]{3,2,1,0:T(8,128)(2,1)} %param.14) | copy-start | bytes 1572868
  167.4 108.3 %copy-start.1 = (bf16[64,1024]{1,0:T(8,128)(2,1)S(1)}, bf16[64,1024]{1,0:T(8,128)(2,1)}, u32[]{:S(2)}) copy-start(bf16[64,1024]{1,0:T(8,128)(2,1)} %param.12) | copy-start | bytes 393220
  204.5 114.6 %all-gather.5.cloned.1.call-start = ((), (), s32[]{:S(2)}) async-start(), calls=%async_computation.6 | async-start | bytes 1179648 | tf_op jit(solution)/shard_map/all_gather | solution.py:58
  277.3 121.2 %reduce-scatter.5.cloned.1.call-start = ((), (), s32[]{:S(2)}) async-start(), calls=%async_computation.7 | async-start | bytes 1179648 | tf_op jit(solution)/shard_map/reduce_scatter | solution.py:102
  321.7 76.7 %copy-start = (bf16[64,1024]{1,0:T(8,128)(2,1)S(1)}, bf16[64,1024]{1,0:T(8,128)(2,1)}, u32[]{:S(2)}) copy-start(bf16[64,1024]{1,0:T(8,128)(2,1)} %add_convert_fusion.1) | copy-start | bytes 393220
Sparse Core Ops, SparseCore 0:
  32.7 107.5 all-gather.2
  204.6 71.0 reduce-scatter.2
  277.7 41.2 all-gather.4
  358.9 39.4 reduce-scatter.4
